TPU v7x, 32 devices: a whole 2x2x4 slice. The times are simulated.
32 devices in a mesh: groups: 2 (over y), col: 4 (over z), row: 2 (over x), sub: 2 (over core).
Axes of the slice: x: 2, y: 2, z: 4, core: 2. Of those that a mesh axis runs over, the one named last changes fastest.
Arguments:
- integrals: bfloat16 [32768, 16384], P(('groups', 'row', 'sub'), 'col'), parts along dimension 0, may hold values from -0.046875 to 0.046875
- integral_mask: int32 [256, 128], P(('groups', 'row', 'sub'), 'col'), parts along dimension 0, may hold values 0 or 1
- amplitudes: bfloat16 [32768, 512], P(('groups', 'col'), ('row', 'sub')), parts along dimension 0, may hold values from -6 to 6
- amplitude_mask: int32 [256, 4], P(('groups', 'col'), ('row', 'sub')), parts along dimension 0, may hold values 0 or 1
- tile_map: int32 [128], replicated, may hold values from 0 to 127, as said below
- row_gap: float32 [32768], P(('groups', 'row', 'sub')), parts along dimension 0, may hold values from 0.3 to 3
- col_gap: float32 [1024], P(('groups', 'col')), parts along dimension 0, may hold values from 0.3 to 3
Outputs:
- cycle_update: bfloat16 [32768, 512], P(('groups', 'row', 'sub'), 'col'), parts along dimension 0
There are 2 independent parts, one for each index of `groups`. A program takes and returns all parts, laid end to end along the dimension named above; an argument that names none is the same for every part. Nothing has to cross between parts.
Inputs may be any that keep to these rules, and one draw needn't show every extreme that they name: tile_map is a permutation of the 128 row tiles. Taking the pair-order row tiles in 4 aligned blocks of 32 and the particle-hole row tiles likewise, every pair block sends exactly max(1, 8) tiles to each particle-hole block that it sends any to, and every particle-hole block receives 128 / 4 tiles.
All inputs are finite; a program needn't handle non-finite values. No bound on the sum of `integral_mask` or of `amplitude_mask` on one device may be relied on, other than what follows from the above.
Results may differ from a plain program's by a relative error of at most 0.012.
Values may be sent and summed in bfloat16 or wider, within the bound.
A program may use at most 128 MiB of HBM per device.

v0:
```python
import jax
import jax.numpy as jnp
from jax import lax
from jax.sharding import PartitionSpec as P

TILE = 128


def per_device(integrals, integral_mask, amplitudes, amplitude_mask, tile_map, row_gap, col_gap):
    position = lax.axis_index("col")
    held_tiles = amplitudes.shape[0] // TILE
    cols_dev = amplitudes.shape[1]
    jt_local = cols_dev // TILE
    total_tiles = tile_map.shape[0]
    shaped = amplitudes.reshape(held_tiles, TILE, jt_local, TILE)
    masked = jnp.where((amplitude_mask > 0)[:, None, :, None], shaped, jnp.zeros_like(shaped))
    masked = masked.reshape(held_tiles, TILE, cols_dev)
    wanted = position * held_tiles + jnp.arange(held_tiles, dtype=jnp.int32)
    matches = tile_map[None, :] == wanted[:, None]
    all_index = jnp.arange(total_tiles, dtype=jnp.int32)
    source = jnp.sum(jnp.where(matches, all_index[None, :], 0), axis=1)
    gathered = lax.all_gather(masked, "col", axis=0, tiled=True)
    relaid = jnp.take(gathered, source, axis=0)
    slab_rows = relaid.reshape(held_tiles * TILE, cols_dev)
    row_tiles = integral_mask.shape[0]
    col_tiles = integral_mask.shape[1]
    tiled = integrals.reshape(row_tiles, TILE, col_tiles, TILE)
    weighted = jnp.where((integral_mask > 0)[:, None, :, None], tiled, jnp.zeros_like(tiled))
    weighted = weighted.reshape(integrals.shape[0], integrals.shape[1])
    partial_value = jnp.dot(
        weighted,
        lax.all_gather(slab_rows, ("row", "sub"), axis=1, tiled=True),
        preferred_element_type=jnp.float32,
    )
    summed = lax.psum_scatter(
        partial_value.astype(jnp.bfloat16), "col", scatter_dimension=1, tiled=True
    ).astype(jnp.float32)
    scaled = summed / (row_gap[:, None] + col_gap[None, :])
    return scaled.astype(jnp.bfloat16)


def solution(mesh):
    return jax.shard_map(
        per_device,
        mesh=mesh,
        in_specs=(
            P(("groups", "row", "sub"), "col"),
            P(("groups", "row", "sub"), "col"),
            P(("groups", "col"), ("row", "sub")),
            P(("groups", "col"), ("row", "sub")),
            P(),
            P(("groups", "row", "sub")),
            P(("groups", "col")),
        ),
        out_specs=P(("groups", "row", "sub"), "col"),
        check_vma=False,
    )
```

profile of v0, /device:TPU:0, one launch (start us, length us, event | category | flops | bytes accessed | tf_op | source)
XLA Modules:
  0.0 259.8 jit_solution(6058563467012482542)
XLA Ops:
  6.5 0.0 all-gather.3.cloned.1.call-start
  6.5 0.7 compare_bitcast_fusion
  7.2 0.0 copy-start.1
  7.2 2.3 broadcast_select_fusion
  9.5 0.0 all-gather.3.cloned.1.call-update
  9.6 0.0 all-gather.5.cloned.1.call-start
  9.6 0.8 select_reduce_fusion
  10.5 0.1 broadcast_bitcast_fusion
  10.6 82.6 %all-gather.3.cloned.1.call-done = bf16[128,128,128]{2,1,0:T(8,128)(2,1)} async-done(((bf16[32,128,128]{2,1,0:T(8,128)(2,1)}), bf16[128,128,128]{2,1,0:T(8,128)(2,1)}) %all-gather.3.cloned.1.call-update) | async-done | bytes 4194320 | tf_op jit(solution)/shard_map/all_gather | solution.py:22
  93.2 2.9 %gather_fusion = bf16[32,128,128]{2,1,0:T(8,128)(2,1)S(1)} fusion(bf16[128,128,128]{2,1,0:T(8,128)(2,1)} %all-gather.3.cloned.1.call-done, s32[1024]{0:T(1024)S(1)} %pad_clamp_fusion), kind=kCustom, calls=%fused_computation | custom fusion | bytes 2097280 | tf_op jit(solution)/shard_map/jit(_take)/gather | solution.py:23
  96.1 2.9 %bitcast_select_fusion.4 = bf16[4096,128]{1,0:T(8,128)(2,1)} fusion(bf16[32,128,128]{2,1,0:T(8,128)(2,1)S(1)} %gather_fusion, pred[4096]{0:T(1024)(128)(4,1)S(1)} %broadcast_bitcast_fusion), kind=kLoop, calls=%fused_computation.6 | loop fusion | flops 524288 | bytes 2101248 | tf_op jit(solution)/shard_map/jit(_take)/select_n | solution.py:23
  99.0 0.0 all-gather.5.cloned.1.call-update
  99.0 0.0 reduce-scatter.4.cloned.1.call-start
  99.1 0.0 copy-done.1
  99.1 33.6 %all-gather.5.cloned.1.call-done = bf16[4096,512]{1,0:T(8,128)(2,1)} async-done(((bf16[4096,128]{1,0:T(8,128)(2,1)}), bf16[4096,512]{1,0:T(8,128)(2,1)}) %all-gather.5.cloned.1.call-update) | async-done | bytes 4194320 | tf_op jit(solution)/shard_map/all_gather | solution.py:32
  132.7 6.7 %broadcast_in_dim.59 = pred[32,128,32,128]{3,2,1,0:T(32,128)(4,1)} broadcast(pred[32,32]{1,0:T(8,128)(4,1)S(1)} %broadcast_compare_fusion), dimensions={0,2} | broadcast | bytes 16778240 | tf_op jit(solution)/shard_map/jit(_where)/broadcast_in_dim | solution.py:28
  139.5 27.3 %fusion.2 = bf16[4096,512]{1,0:T(8,128)(2,1)} fusion(bf16[4096,512]{1,0:T(8,128)(2,1)} %all-gather.5.cloned.1.call-done, bf16[4096,4096]{1,0:T(8,128)(2,1)} %param.7, pred[512,8,32,128]{3,2,1,0:T(32,128)(4,1)} %bitcast.21), kind=kOutput, calls=%fused_computation.4 | convolution fusion | flops 17198743552 | bytes 58720256 | tf_op jit(solution)/shard_map/dot_general | solution.py:30
  166.7 6.4 %copy.8 = bf16[4096,512]{0,1:T(8,128)(2,1)} copy(bf16[4096,512]{1,0:T(8,128)(2,1)} %fusion.2) | data formatting | bytes 8388608
  173.2 0.0 copy-start
  173.2 0.0 copy-start.2
  173.2 0.0 reduce-scatter.4.cloned.1.call-update
  173.2 76.9 %reduce-scatter.4.cloned.1.call-done = bf16[128,4096]{1,0:T(8,128)(2,1)} async-done(((bf16[512,4096]{1,0:T(8,128)(2,1)}), bf16[128,4096]{1,0:T(8,128)(2,1)}) %reduce-scatter.4.cloned.1.call-update) | async-done | bytes 1048592
  250.1 1.6 copy.9
  251.8 0.0 copy-done
  251.8 0.0 copy-done.2
  251.8 1.5 divide_convert_fusion
  (5 shorter events, 0.0 us)
Async XLA Ops:
  6.5 86.7 %all-gather.3.cloned.1.call-start = ((), (), s32[]{:S(2)}) async-start(), calls=%async_computation.1 | async-start | bytes 5242880 | tf_op jit(solution)/shard_map/all_gather | solution.py:22
  7.2 91.9 %copy-start.1 = (s32[32,32]{1,0:T(8,128)S(1)}, s32[32,32]{1,0:T(8,128)}, u32[]{:S(2)}) copy-start(s32[32,32]{1,0:T(8,128)} %param.8) | copy-start | bytes 12292
  9.6 123.2 %all-gather.5.cloned.1.call-start = ((), (), s32[]{:S(2)}) async-start(), calls=%async_computation.2 | async-start | bytes 5242880 | tf_op jit(solution)/shard_map/all_gather | solution.py:32
  99.0 151.1 %reduce-scatter.4.cloned.1.call-start = ((), (), s32[]{:S(2)}) async-start(), calls=%async_computation.3 | async-start | bytes 5242880
  173.2 78.6 %copy-start = (f32[4096]{0:T(1024)S(1)}, f32[4096]{0:T(1024)}, u32[]{:S(2)}) copy-start(f32[4096]{0:T(1024)} %param.12) | copy-start | bytes 49156
  173.2 78.6 %copy-start.2 = (f32[128]{0:T(128)S(1)}, f32[128]{0:T(128)}, u32[]{:S(2)}) copy-start(f32[128]{0:T(128)} %param.13) | copy-start | bytes 1540
Sparse Core Ops, SparseCore 0:
  9.7 83.4 all-gather.2
  99.2 33.5 all-gather.4
  173.3 76.7 reduce-scatter.3
where the time goes:
time: 260 us
  waiting for transfers between devices  193 us (74%)
  matrix products  27.3 us (10%)
  local copies, waits for them, and re-layouts  17.8 us (7%)
  between operations  13.2 us (5%)
  other arithmetic  8.27 us (3%)
    all_gather x1, waiting for transfers between devices, per_device(): gathered = lax.all_gather(masked, 'col', axis=0, tiled=True)  82.6 us
    unnamed x4, waiting for transfers between devices  77 us
    all_gather x1, waiting for transfers between devices, per_device(): lax.all_gather(slab_rows, ('row', 'sub'), axis=1, tiled=True)  33.6 us
    dot_general x1, matrix products, per_device(): jnp.dot(weighted, lax.all_gather(slab_rows, ('row', 'sub'), axis=1, tiled...  27.3 us
    unnamed x8, local copies, waits for them, and re-layouts  8.09 us
    broadcast_in_dim x1, local copies, waits for them, and re-layouts, per_device(): jnp.where((integral_mask > 0)[:, None, :, None], tiled, jnp.zeros_like(ti...  6.72 us
  transfers between devices with their start and end apart: 3, of which 3 were waited for; matrix products, arithmetic and copies ran while one was open for 0% of the time, Pallas kernels for 0%

commit v1 on v0

v1 whole, which is shorter than its diff:
```python
import functools

import jax
import jax.numpy as jnp
from jax import lax
from jax.experimental import pallas as pl
from jax.experimental.pallas import tpu as pltpu
from jax.sharding import PartitionSpec as P

TILE = 128
MESH = pl.DeviceIdType.MESH


def largest_block(size, most):
    block = min(size, most)
    while size % block:
        block -= TILE
    return block


def kernel(
    n_col, n_row, n_sub, cap,
    index_ref, mask_ref, amp_ref, row_gap_ref, col_gap_ref, w_ref,
    out_ref,
    w_buf, send_buf, recv_buf, slab, part, sums,
    w_sem, a_send, a_recv, b_send, b_recv, s_send, s_recv,
):
    col = lax.axis_index("col")
    row = lax.axis_index("row")
    sub = lax.axis_index("sub")
    here = row * n_sub + sub
    n_j = n_row * n_sub
    rows, depth = w_buf.shape
    held = depth // TILE
    width = part.shape[2]
    block = largest_block(rows, 256)
    n_block = rows // block
    mm_block = largest_block(rows, 512)
    n_mm = rows // mm_block
    n_w = w_sem.shape[0]
    w_part = rows // n_w

    def w_copy(k):
        view = pl.ds(pl.multiple_of(k * w_part, TILE), w_part)
        return pltpu.make_async_copy(w_ref.at[view], w_buf.at[view], w_sem.at[k])

    for k in range(n_w):
        w_copy(k).start()

    barrier = pltpu.get_barrier_semaphore()
    for k in range(1, n_col):
        pl.semaphore_signal(barrier, inc=1, device_id={"col": (col + k) % n_col}, device_id_type=MESH)
    for k in range(1, n_row):
        pl.semaphore_signal(barrier, inc=1, device_id={"row": (row + k) % n_row}, device_id_type=MESH)
    for k in range(1, n_sub):
        pl.semaphore_signal(barrier, inc=1, device_id={"sub": (sub + k) % n_sub}, device_id_type=MESH)

    @pl.loop(0, n_col * cap)
    def _(q):
        keep = index_ref[n_col * cap + held + q].astype(jnp.float32)
        tile = amp_ref[index_ref[q]].astype(jnp.float32)
        send_buf[q] = (tile * keep).astype(jnp.bfloat16)

    pl.semaphore_wait(barrier, n_col - 1 + n_row - 1 + n_sub - 1)

    def rows_of(s):
        return pl.ds(s * cap, cap)

    def a_copy(k):
        target = (col + k) % n_col
        return pltpu.make_async_remote_copy(
            src_ref=send_buf.at[rows_of(target)],
            dst_ref=recv_buf.at[here, rows_of(col)],
            send_sem=a_send.at[k],
            recv_sem=a_recv.at[k],
            device_id={"col": target},
            device_id_type=MESH,
        )

    def spread(j, s, slot, device):
        return pltpu.make_async_remote_copy(
            src_ref=recv_buf.at[j, rows_of(s)],
            dst_ref=recv_buf.at[j, rows_of(s)],
            send_sem=b_send.at[slot, s],
            recv_sem=b_recv.at[j, s],
            device_id=device,
            device_id_type=MESH,
        )

    for k in range(1, n_col):
        a_copy(k).start()
    recv_buf[here, rows_of(col)] = send_buf[rows_of(col)]

    lane_tile = lax.broadcasted_iota(jnp.int32, (held, depth), 1) // TILE
    tile_row = lax.broadcasted_iota(jnp.int32, (held, depth), 0)
    expand = jnp.where(lane_tile == tile_row, 1.0, 0.0).astype(jnp.bfloat16)
    wide_mask = jnp.dot(
        mask_ref[...].astype(jnp.bfloat16), expand, preferred_element_type=jnp.float32
    ).astype(jnp.bfloat16)

    row_tiles = rows // TILE
    part_tiles = w_part // TILE

    def screen(k):
        w_copy(k).wait()
        for i in range(part_tiles):
            it = k * part_tiles + i
            keep = jnp.broadcast_to(wide_mask[it : it + 1, :], (16, depth))

            @pl.loop(0, TILE // 16)
            def _(r):
                view = pl.ds(pl.multiple_of(it * TILE + r * 16, 16), 16)
                w_buf[view, :] = w_buf[view, :] * keep

    def source(k):
        return (col + n_col - k) % n_col

    def relay(k):
        s = source(k)
        for r in range(1, n_row):
            j = ((row + r) % n_row) * n_sub + sub
            spread(j, s, 0, {"row": row} if n_sub == 1 else {"sub": (sub + 1) % n_sub}).wait_recv()
            for u in range(1, n_sub):
                spread(j, s, n_row - 1 + r * (n_sub - 1) + u - 1, {"sub": (sub + u) % n_sub}).start()

    for k in range(n_col):
        s = source(k)
        if k > 0:
            a_copy(k).wait_recv()
        for r in range(1, n_row):
            spread(here, s, r - 1, {"row": (row + r) % n_row}).start()
        for u in range(1, n_sub):
            spread(here, s, n_row - 1 + u - 1, {"sub": (sub + u) % n_sub}).start()
        if k < n_w:
            screen(k)
        if k > 0:
            relay(k - 1)
    relay(n_col - 1)
    for k in range(n_col):
        s = source(k)
        for u in range(1, n_sub):
            for r in range(n_row):
                j = ((row + r) % n_row) * n_sub + (sub + u) % n_sub
                spread(j, s, 0, {"sub": (sub + 1) % n_sub}).wait_recv()

    @pl.loop(0, held)
    def _(k):
        slot = index_ref[n_col * cap + k]
        for j in range(n_j):
            slab[pl.ds(pl.multiple_of(k * TILE, TILE), TILE), j * TILE : (j + 1) * TILE] = recv_buf[j, slot]

    def s_copy(t, m, right):
        view = pl.ds(pl.multiple_of(m * block, TILE), block)
        return pltpu.make_async_remote_copy(
            src_ref=part.at[t, view],
            dst_ref=sums.at[0 if right else 1, t, view],
            send_sem=s_send.at[t, m],
            recv_sem=s_recv.at[0 if right else 1, t, m],
            device_id={"col": (col + (1 if right else n_col - 1)) % n_col},
            device_id_type=MESH,
        )

    n_cols = n_col * width
    n_wide = largest_block(n_cols, 256)

    @pl.loop(0, n_mm)
    def _(m):
        view = pl.ds(pl.multiple_of(m * mm_block, TILE), mm_block)
        for n in range(n_cols // n_wide):
            product = jnp.dot(
                w_buf[view, :], slab[:, n * n_wide : (n + 1) * n_wide], preferred_element_type=jnp.float32
            ).astype(jnp.bfloat16)
            for t in range(n_wide // width):
                part[n * (n_wide // width) + t, view, :] = product[:, t * width : (t + 1) * width]
        for i in range(mm_block // block):
            at = m * (mm_block // block) + i

            @pl.when(col == 0)
            def _():
                for t in range(n_col - 1, 0, -1):
                    s_copy(t, at, True).start()

            @pl.when(col == n_col - 1)
            def _():
                for t in range(n_col - 1):
                    s_copy(t, at, False).start()

    inner = jnp.logical_and(col > 0, col < n_col - 1)

    @pl.loop(0, n_block)
    def _(m):
        view = pl.ds(pl.multiple_of(m * block, TILE), block)
        for t in range(n_col - 1, 0, -1):

            @pl.when(jnp.logical_and(inner, col < t))
            def _():
                s_copy(t, m, True).wait_recv()
                total = part[t, view, :].astype(jnp.float32) + sums[0, t, view, :].astype(jnp.float32)
                part[t, view, :] = total.astype(jnp.bfloat16)
                s_copy(t, m, True).start()

        for t in range(n_col - 1):

            @pl.when(jnp.logical_and(inner, col > t))
            def _():
                s_copy(t, m, False).wait_recv()
                total = part[t, view, :].astype(jnp.float32) + sums[1, t, view, :].astype(jnp.float32)
                part[t, view, :] = total.astype(jnp.bfloat16)
                s_copy(t, m, False).start()

        def gaps():
            pieces = []
            for i in range(block // TILE):
                line = row_gap_ref[pl.ds(m * (block // TILE) + i, 1), :]
                pieces.append(jnp.broadcast_to(line, (TILE, TILE)).T)
            return jnp.concatenate(pieces, axis=0) + col_gap_ref[...]

        @pl.when(col == 0)
        def _():
            s_copy(0, m, False).wait_recv()
            total = part[0, view, :].astype(jnp.float32) + sums[1, 0, view, :].astype(jnp.float32)
            out_ref[view, :] = (total / gaps()).astype(jnp.bfloat16)

        @pl.when(col == n_col - 1)
        def _():
            s_copy(n_col - 1, m, True).wait_recv()
            total = part[n_col - 1, view, :].astype(jnp.float32) + sums[0, n_col - 1, view, :].astype(jnp.float32)
            out_ref[view, :] = (total / gaps()).astype(jnp.bfloat16)

        @pl.when(inner)
        def _():
            s_copy(col, m, True).wait_recv()
            s_copy(col, m, False).wait_recv()
            total = part[col, view, :].astype(jnp.float32) + sums[0, col, view, :].astype(jnp.float32)
            total = total + sums[1, col, view, :].astype(jnp.float32)
            out_ref[view, :] = (total / gaps()).astype(jnp.bfloat16)

    for k in range(1, n_col):
        a_copy(k).wait_send()
    for k in range(n_col):
        for slot in range(n_row - 1 + n_row * (n_sub - 1)):
            spread(here, k, slot, {"sub": (sub + 1) % n_sub}).wait_send()

    @pl.loop(0, n_block)
    def _(m):
        for t in range(n_col):

            @pl.when(col != t)
            def _():
                s_copy(t, m, True).wait_send()


def per_device(integrals, integral_mask, amplitudes, amplitude_mask, tile_map, row_gap, col_gap, *, n_row, n_sub):
    position = lax.axis_index("col")
    held = amplitudes.shape[0] // TILE
    total = tile_map.shape[0]
    n_col = total // held
    cap = max(1, held // n_col)
    width = col_gap.shape[0]
    rows, depth = integrals.shape
    n_j = n_row * n_sub
    n_block = rows // largest_block(rows, 256)

    every = jnp.arange(total, dtype=jnp.int32)
    owner = tile_map // held
    home = every // held
    earlier = (home[:, None] == home[None, :]) & (owner[:, None] == owner[None, :]) & (every[:, None] < every[None, :])
    rank = jnp.sum(earlier.astype(jnp.int32), axis=0)
    slots = n_col * cap
    line = jnp.arange(2 * slots + held, dtype=jnp.int32)[:, None]
    sent = (home == position)[None, :] & ((owner * cap + rank)[None, :] == line % (slots + held))
    kept = jnp.tile(amplitude_mask.reshape(held), n_col)
    landed = tile_map[None, :] == position * held + line - slots
    index = jnp.sum(
        jnp.where(
            line < slots,
            jnp.where(sent, (every % held)[None, :], 0),
            jnp.where(
                line < slots + held,
                jnp.where(landed, (home * cap + rank)[None, :], 0),
                jnp.where(sent, kept[None, :], 0),
            ),
        ),
        axis=1,
    )

    smem = pl.BlockSpec(memory_space=pltpu.SMEM)
    vmem = pl.BlockSpec(memory_space=pltpu.VMEM)
    dma = pltpu.SemaphoreType.DMA
    return pl.pallas_call(
        functools.partial(kernel, n_col, n_row, n_sub, cap),
        out_shape=jax.ShapeDtypeStruct((rows, width), jnp.bfloat16),
        in_specs=[smem, vmem, vmem, vmem, vmem, pl.BlockSpec(memory_space=pl.ANY)],
        out_specs=vmem,
        scratch_shapes=[
            pltpu.VMEM((rows, depth), jnp.bfloat16),
            pltpu.VMEM((slots, TILE, TILE), jnp.bfloat16),
            pltpu.VMEM((n_j, slots, TILE, TILE), jnp.bfloat16),
            pltpu.VMEM((depth, n_j * TILE), jnp.bfloat16),
            pltpu.VMEM((n_col, rows, width), jnp.bfloat16),
            pltpu.VMEM((2, n_col, rows, width), jnp.bfloat16),
            dma((min(n_col, rows // TILE),)),
            dma((n_col,)),
            dma((n_col,)),
            dma((n_row - 1 + n_row * (n_sub - 1), n_col)),
            dma((n_j, n_col)),
            dma((n_col, n_block)),
            dma((2, n_col, n_block)),
        ],
        compiler_params=pltpu.CompilerParams(
            collective_id=0, has_side_effects=True, vmem_limit_bytes=62 * 1024 * 1024
        ),
        cost_estimate=pl.CostEstimate(
            flops=2 * rows * depth * n_j * TILE, bytes_accessed=2 * rows * depth, transcendentals=0
        ),
    )(
        index,
        integral_mask,
        amplitudes.reshape(held, TILE, TILE),
        row_gap.reshape(rows // TILE, TILE),
        col_gap.reshape(1, width),
        integrals,
    )


def solution(mesh):
    return jax.shard_map(
        functools.partial(per_device, n_row=mesh.shape["row"], n_sub=mesh.shape["sub"]),
        mesh=mesh,
        in_specs=(
            P(("groups", "row", "sub"), "col"),
            P(("groups", "row", "sub"), "col"),
            P(("groups", "col"), ("row", "sub")),
            P(("groups", "col"), ("row", "sub")),
            P(),
            P(("groups", "row", "sub")),
            P(("groups", "col")),
        ),
        out_specs=P(("groups", "row", "sub"), "col"),
        check_vma=False,
    )
```

time: 260 us -> 194 us (0.75)
  waiting for transfers between devices: 193 us -> 0 us
  Pallas kernels: 0 us -> 189 us
  matrix products: 27.3 us -> 0 us
  local copies, waits for them, and re-layouts: 17.8 us -> 3.01 us
  between operations: 13.2 us -> 0.02 us
  other arithmetic: 8.27 us -> 2.2 us
    pallas_call x0 -> x1, Pallas kernels: none -> 189 us  [per_device(): pl.pallas_call(functools.partial(kernel, n_col, n_row, n_sub, cap), out_s...]
    all_gather x2 -> x0, waiting for transfers between devices: 116 us -> none  [the longest x1 82.6 us: per_device(): gathered = lax.all_gather(masked, 'col', axis=0, tiled=True)]
    unnamed x4 -> x0, waiting for transfers between devices: 77 us -> none
    dot_general x1 -> x0, matrix products: 27.3 us -> none  [per_device(): jnp.dot(weighted, lax.all_gather(slab_rows, ('row', 'sub'), axis=1, tiled...]
    broadcast_in_dim x2 -> x1, local copies, waits for them, and re-layouts: 6.8 us -> 0.08 us  [per_device(): jnp.where(sent, kept[None, :], 0)]
    unnamed x8 -> x1, local copies, waits for them, and re-layouts: 8.09 us -> 2.26 us
    select_n x3, other arithmetic: 5.24 us -> 0.67 us  [the longest x1 0.67 us: per_device(): owner = tile_map // held]
    gather x1 -> x0, local copies, waits for them, and re-layouts: 2.93 us -> none  [per_device(): relaid = jnp.take(gathered, source, axis=0)]
  transfers between devices with their start and end apart: 3 -> 0, of which waited for: 3 -> 0; matrix products, arithmetic and copies ran while one was open for 0% -> 0% of each run, Pallas kernels for 0% -> 0%
where the time goes in v1:
time: 194 us
  Pallas kernels  189 us (97%)
  local copies, waits for them, and re-layouts  3.01 us (2%)
  other arithmetic  2.2 us (1%)
    pallas_call x1, Pallas kernels, per_device(): pl.pallas_call(functools.partial(kernel, n_col, n_row, n_sub, cap), out_s...  189 us

profile of v1, /device:TPU:0, one launch (start us, length us, event | category | flops | bytes accessed | tf_op | source)
XLA Modules:
  0.0 194.2 jit_solution(6213228492718925216)
XLA Ops:
  0.0 0.7 and_select_fusion.2
  0.7 0.1 convert_reduce_fusion
  0.8 0.7 tile.8
  1.5 0.1 broadcast_in_dim.56
  1.6 1.4 select_reduce_fusion.index_ref
  3.0 189.0 %shard_map.73 = bf16[4096,128]{1,0:T(8,128)(2,1)} custom-call(s32[96]{0:T(128)} %select_reduce_fusion.index_ref, s32[32,32]{1,0:T(8,128)} %mask_ref.1, bf16[32,128,128]{2,1,0:T(8,128)(2,1)} %bitcast.5, f32[32,128]{1,0:T(8,128)} %bitcast.6, f32[1,128]{1,0:T(1,128)} %bitcast.7, bf16[4096,4096]{1,0:T(8,128)(2,1)} %w_ref.1), custom_call_target="tpu_custom_call" | custom-call | flops 17179869184 | bytes 33554432 | tf_op jit(solution)/shard_map/pallas_call | solution.py:290
  192.0 2.3 %copy.9 = bf16[4096,128]{1,0:T(8,128)(2,1)} copy(bf16[4096,128]{1,0:T(8,128)(2,1)} %shard_map.73) | data formatting | bytes 2097152
  (5 shorter events, 0.0 us)

commit v2 on v1

--- a/solution.py
+++ b/solution.py
@@ -36,7 +36,6 @@
     block = largest_block(rows, 256)
     n_block = rows // block
     mm_block = largest_block(rows, 512)
-    n_mm = rows // mm_block
     n_w = w_sem.shape[0]
     w_part = rows // n_w
 
@@ -66,13 +65,20 @@
     def rows_of(s):
         return pl.ds(s * cap, cap)
 
-    def a_copy(k):
-        target = (col + k) % n_col
+    nearest = [sorted(range(n_col), key=lambda s: (abs(s - c), abs(2 * s + 1 - n_col))) for c in range(n_col)]
+
+    def source(k):
+        found = col * 0
+        for c in range(n_col):
+            found = jnp.where(col == c, nearest[c][k], found)
+        return found
+
+    def a_copy(target, origin):
         return pltpu.make_async_remote_copy(
             src_ref=send_buf.at[rows_of(target)],
             dst_ref=recv_buf.at[here, rows_of(col)],
-            send_sem=a_send.at[k],
-            recv_sem=a_recv.at[k],
+            send_sem=a_send.at[target],
+            recv_sem=a_recv.at[origin],
             device_id={"col": target},
             device_id_type=MESH,
         )
@@ -88,7 +94,7 @@
         )
 
     for k in range(1, n_col):
-        a_copy(k).start()
+        a_copy(source(k), col).start()
     recv_buf[here, rows_of(col)] = send_buf[rows_of(col)]
 
     lane_tile = lax.broadcasted_iota(jnp.int32, (held, depth), 1) // TILE
@@ -111,9 +117,6 @@
             def _(r):
                 view = pl.ds(pl.multiple_of(it * TILE + r * 16, 16), 16)
                 w_buf[view, :] = w_buf[view, :] * keep
-
-    def source(k):
-        return (col + n_col - k) % n_col
 
     def relay(k):
         s = source(k)
@@ -126,7 +129,7 @@
     for k in range(n_col):
         s = source(k)
         if k > 0:
-            a_copy(k).wait_recv()
+            a_copy(s, s).wait_recv()
         for r in range(1, n_row):
             spread(here, s, r - 1, {"row": (row + r) % n_row}).start()
         for u in range(1, n_sub):
@@ -163,80 +166,94 @@
     n_cols = n_col * width
     n_wide = largest_block(n_cols, 256)
 
-    @pl.loop(0, n_mm)
-    def _(m):
-        view = pl.ds(pl.multiple_of(m * mm_block, TILE), mm_block)
-        for n in range(n_cols // n_wide):
-            product = jnp.dot(
-                w_buf[view, :], slab[:, n * n_wide : (n + 1) * n_wide], preferred_element_type=jnp.float32
-            ).astype(jnp.bfloat16)
-            for t in range(n_wide // width):
-                part[n * (n_wide // width) + t, view, :] = product[:, t * width : (t + 1) * width]
-        for i in range(mm_block // block):
-            at = m * (mm_block // block) + i
-
-            @pl.when(col == 0)
+    inner = jnp.logical_and(col > 0, col < n_col - 1)
+    per_mm = mm_block // block
+
+    def gaps(m):
+        pieces = []
+        for i in range(block // TILE):
+            line = row_gap_ref[pl.ds(m * (block // TILE) + i, 1), :]
+            pieces.append(jnp.broadcast_to(line, (TILE, TILE)).T)
+        return jnp.concatenate(pieces, axis=0) + col_gap_ref[...]
+
+    def relay_sums(m, right):
+        view = pl.ds(pl.multiple_of(m * block, TILE), block)
+        for t in range(n_col - 1, 0, -1) if right else range(n_col - 1):
+
+            @pl.when(col < t if right else col > t)
             def _():
-                for t in range(n_col - 1, 0, -1):
-                    s_copy(t, at, True).start()
-
-            @pl.when(col == n_col - 1)
-            def _():
-                for t in range(n_col - 1):
-                    s_copy(t, at, False).start()
-
-    inner = jnp.logical_and(col > 0, col < n_col - 1)
-
-    @pl.loop(0, n_block)
-    def _(m):
+                s_copy(t, m, right).wait_recv()
+                total = part[t, view, :].astype(jnp.float32) + sums[0 if right else 1, t, view, :].astype(jnp.float32)
+                part[t, view, :] = total.astype(jnp.bfloat16)
+                s_copy(t, m, right).start()
+
+    def finish(m, from_left, from_right):
         view = pl.ds(pl.multiple_of(m * block, TILE), block)
-        for t in range(n_col - 1, 0, -1):
-
-            @pl.when(jnp.logical_and(inner, col < t))
-            def _():
-                s_copy(t, m, True).wait_recv()
-                total = part[t, view, :].astype(jnp.float32) + sums[0, t, view, :].astype(jnp.float32)
-                part[t, view, :] = total.astype(jnp.bfloat16)
-                s_copy(t, m, True).start()
-
-        for t in range(n_col - 1):
-
-            @pl.when(jnp.logical_and(inner, col > t))
-            def _():
-                s_copy(t, m, False).wait_recv()
-                total = part[t, view, :].astype(jnp.float32) + sums[1, t, view, :].astype(jnp.float32)
-                part[t, view, :] = total.astype(jnp.bfloat16)
-                s_copy(t, m, False).start()
-
-        def gaps():
-            pieces = []
-            for i in range(block // TILE):
-                line = row_gap_ref[pl.ds(m * (block // TILE) + i, 1), :]
-                pieces.append(jnp.broadcast_to(line, (TILE, TILE)).T)
-            return jnp.concatenate(pieces, axis=0) + col_gap_ref[...]
-
-        @pl.when(col == 0)
-        def _():
-            s_copy(0, m, False).wait_recv()
-            total = part[0, view, :].astype(jnp.float32) + sums[1, 0, view, :].astype(jnp.float32)
-            out_ref[view, :] = (total / gaps()).astype(jnp.bfloat16)
-
-        @pl.when(col == n_col - 1)
-        def _():
-            s_copy(n_col - 1, m, True).wait_recv()
-            total = part[n_col - 1, view, :].astype(jnp.float32) + sums[0, n_col - 1, view, :].astype(jnp.float32)
-            out_ref[view, :] = (total / gaps()).astype(jnp.bfloat16)
-
-        @pl.when(inner)
-        def _():
+        total = part[col, view, :].astype(jnp.float32)
+        if from_left:
             s_copy(col, m, True).wait_recv()
+            total = total + sums[0, col, view, :].astype(jnp.float32)
+        if from_right:
             s_copy(col, m, False).wait_recv()
-            total = part[col, view, :].astype(jnp.float32) + sums[0, col, view, :].astype(jnp.float32)
             total = total + sums[1, col, view, :].astype(jnp.float32)
-            out_ref[view, :] = (total / gaps()).astype(jnp.bfloat16)
+        out_ref[view, :] = (total / gaps(m)).astype(jnp.bfloat16)
+
+    lag = 3
+    right_lag = lag * (col - 1)
+    left_lag = lag * (n_col - 2 - col)
+    last_lag = lag * (n_col - 2)
+
+    @pl.loop(0, n_block + last_lag)
+    def _(step):
+        @pl.when(jnp.logical_and(step < n_block, step % per_mm == 0))
+        def _():
+            view = pl.ds(pl.multiple_of(step * block, TILE), mm_block)
+            for n in range(n_cols // n_wide):
+                product = jnp.dot(
+                    w_buf[view, :], slab[:, n * n_wide : (n + 1) * n_wide], preferred_element_type=jnp.float32
+                ).astype(jnp.bfloat16)
+                for t in range(n_wide // width):
+                    part[n * (n_wide // width) + t, view, :] = product[:, t * width : (t + 1) * width]
+
+        @pl.when(jnp.logical_and(step < n_block, col == 0))
+        def _():
+            for t in range(n_col - 1, 0, -1):
+                s_copy(t, step, True).start()
+
+        @pl.when(jnp.logical_and(step < n_block, col == n_col - 1))
+        def _():
+            for t in range(n_col - 1):
+                s_copy(t, step, False).start()
+
+        def within(m):
+            return jnp.logical_and(inner, jnp.logical_and(m >= 0, m < n_block))
+
+        @pl.when(within(step - right_lag))
+        def _():
+            relay_sums(step - right_lag, True)
+
+        @pl.when(within(step - left_lag))
+        def _():
+            relay_sums(step - left_lag, False)
+
+        @pl.when(within(step - last_lag))
+        def _():
+            finish(step - last_lag, True, True)
+
+    @pl.when(col == 0)
+    def _():
+        @pl.loop(0, n_block)
+        def _(m):
+            finish(m, False, True)
+
+    @pl.when(col == n_col - 1)
+    def _():
+        @pl.loop(0, n_block)
+        def _(m):
+            finish(m, True, False)
 
     for k in range(1, n_col):
-        a_copy(k).wait_send()
+        a_copy(source(k), col).wait_send()
     for k in range(n_col):
         for slot in range(n_row - 1 + n_row * (n_sub - 1)):
             spread(here, k, slot, {"sub": (sub + 1) % n_sub}).wait_send()

time: 194 us -> 130 us (0.67)
  Pallas kernels: 189 us -> 124 us
    pallas_call x1, Pallas kernels: 189 us -> 124 us  [per_device(): pl.pallas_call(functools.partial(kernel, n_col, n_row, n_sub, cap), out_s...]
where the time goes in v2:
time: 130 us; the launch traced here: 129 us
  Pallas kernels  124 us (95%)
  local copies, waits for them, and re-layouts  3.01 us (2%)
  other arithmetic  2.2 us (2%)
    pallas_call x1, Pallas kernels, per_device(): pl.pallas_call(functools.partial(kernel, n_col, n_row, n_sub, cap), out_s...  124 us

profile of v2, /device:TPU:0, one launch (start us, length us, event | category | flops | bytes accessed | tf_op | source)
XLA Modules:
  0.0 129.4 jit_solution(12534841130870103341)
XLA Ops:
  0.0 0.7 and_select_fusion.2
  0.7 0.1 convert_reduce_fusion
  0.8 0.7 tile.8
  1.5 0.1 broadcast_in_dim.56
  1.6 1.4 %select_reduce_fusion.index_ref = s32[96]{0:T(128)} fusion(s32[128]{0:T(128)S(1)} %broadcast_in_dim.56, s32[128]{0:T(128)S(1)} %get-tuple-element.6, s32[128]{0:T(128)} %param.11, s32[128]{0:T(128)S(1)} %and_select_fusion, s32[128]{0:T(128)S(1)} %get-tuple-element.5, s32[96]{0:T(128)S(1)} %get-tuple-element.10, s32[96]{0:T(128)S(1)} %get-tuple-element.9, ...), kind=kLoop, calls=%fused_computation.3 | loop fusion | flops 110496 | bytes 4032 | tf_op jit(solution)/shard_map/reduce_sum | solution.py:291
  3.0 124.2 %shard_map.73 = bf16[4096,128]{1,0:T(8,128)(2,1)} custom-call(s32[96]{0:T(128)} %select_reduce_fusion.index_ref, s32[32,32]{1,0:T(8,128)} %mask_ref.1, bf16[32,128,128]{2,1,0:T(8,128)(2,1)} %bitcast.5, f32[32,128]{1,0:T(8,128)} %bitcast.6, f32[1,128]{1,0:T(1,128)} %bitcast.7, bf16[4096,4096]{1,0:T(8,128)(2,1)} %w_ref.1), custom_call_target="tpu_custom_call" | custom-call | flops 17179869184 | bytes 33554432 | tf_op jit(solution)/shard_map/pallas_call | solution.py:307
  127.2 2.3 %copy.9 = bf16[4096,128]{1,0:T(8,128)(2,1)} copy(bf16[4096,128]{1,0:T(8,128)(2,1)} %shard_map.73) | data formatting | bytes 2097152
  (5 shorter events, 0.0 us)

commit v3 on v2

--- a/solution.py
+++ b/solution.py
@@ -43,8 +43,6 @@
         view = pl.ds(pl.multiple_of(k * w_part, TILE), w_part)
         return pltpu.make_async_copy(w_ref.at[view], w_buf.at[view], w_sem.at[k])
 
-    for k in range(n_w):
-        w_copy(k).start()
 
     barrier = pltpu.get_barrier_semaphore()
     for k in range(1, n_col):
@@ -93,7 +91,7 @@
             device_id_type=MESH,
         )
 
-    for k in range(1, n_col):
+    for k in range(n_col - 1, 0, -1):
         a_copy(source(k), col).start()
     recv_buf[here, rows_of(col)] = send_buf[rows_of(col)]
 
@@ -134,6 +132,9 @@
             spread(here, s, r - 1, {"row": (row + r) % n_row}).start()
         for u in range(1, n_sub):
             spread(here, s, n_row - 1 + u - 1, {"sub": (sub + u) % n_sub}).start()
+        if k == 0:
+            for i in range(n_w):
+                w_copy(i).start()
         if k < n_w:
             screen(k)
         if k > 0:
@@ -198,7 +199,7 @@
             total = total + sums[1, col, view, :].astype(jnp.float32)
         out_ref[view, :] = (total / gaps(m)).astype(jnp.bfloat16)
 
-    lag = 3
+    lag = 2
     right_lag = lag * (col - 1)
     left_lag = lag * (n_col - 2 - col)
     last_lag = lag * (n_col - 2)

time: 130 us -> 126 us (0.969)
  Pallas kernels: 124 us -> 121 us
    pallas_call x1, Pallas kernels: 124 us -> 121 us  [per_device(): pl.pallas_call(functools.partial(kernel, n_col, n_row, n_sub, cap), out_s...]
where the time goes in v3:
time: 126 us
  Pallas kernels  121 us (96%)
  local copies, waits for them, and re-layouts  3.01 us (2%)
  other arithmetic  2.2 us (2%)
    pallas_call x1, Pallas kernels, per_device(): pl.pallas_call(functools.partial(kernel, n_col, n_row, n_sub, cap), out_s...  121 us

profile of v3, /device:TPU:0, one launch (start us, length us, event | category | flops | bytes accessed | tf_op | source)
XLA Modules:
  0.0 125.8 jit_solution(11229657609223165001)
XLA Ops:
  0.0 0.7 and_select_fusion.2
  0.7 0.1 convert_reduce_fusion
  0.8 0.7 tile.8
  1.5 0.1 broadcast_in_dim.56
  1.6 1.4 %select_reduce_fusion.index_ref = s32[96]{0:T(128)} fusion(s32[128]{0:T(128)S(1)} %broadcast_in_dim.56, s32[128]{0:T(128)S(1)} %get-tuple-element.6, s32[128]{0:T(128)} %param.11, s32[128]{0:T(128)S(1)} %and_select_fusion, s32[128]{0:T(128)S(1)} %get-tuple-element.5, s32[96]{0:T(128)S(1)} %get-tuple-element.10, s32[96]{0:T(128)S(1)} %get-tuple-element.9, ...), kind=kLoop, calls=%fused_computation.3 | loop fusion | flops 110496 | bytes 4032 | tf_op jit(solution)/shard_map/reduce_sum | solution.py:292
  3.0 120.5 %shard_map.73 = bf16[4096,128]{1,0:T(8,128)(2,1)} custom-call(s32[96]{0:T(128)} %select_reduce_fusion.index_ref, s32[32,32]{1,0:T(8,128)} %mask_ref.1, bf16[32,128,128]{2,1,0:T(8,128)(2,1)} %bitcast.5, f32[32,128]{1,0:T(8,128)} %bitcast.6, f32[1,128]{1,0:T(1,128)} %bitcast.7, bf16[4096,4096]{1,0:T(8,128)(2,1)} %w_ref.1), custom_call_target="tpu_custom_call" | custom-call | flops 17179869184 | bytes 33554432 | tf_op jit(solution)/shard_map/pallas_call | solution.py:308
  123.5 2.3 %copy.9 = bf16[4096,128]{1,0:T(8,128)(2,1)} copy(bf16[4096,128]{1,0:T(8,128)(2,1)} %shard_map.73) | data formatting | bytes 2097152
  (5 shorter events, 0.0 us)
